TPU v7x, 32 devices: a whole 2x2x4 slice. The times are simulated.
32 devices in a mesh: grp: 2 (over y), row: 4 (over z), head: 2 (over x), sub: 2 (over core).
Axes of the slice: x: 2, y: 2, z: 4, core: 2. Of those that a mesh axis runs over, the one named last changes fastest.
Arguments:
- queries: bfloat16 [4, 96, 32, 1024], P('head', ('grp', 'row')), parts along dimension 1, may hold values from -6 to 6
- key_side: bfloat16 [4, 96, 32, 1024], P('head', ('grp', 'row'), None, 'sub'), parts along dimension 1, may hold values from -6 to 6
- value_side: bfloat16 [4, 96, 32, 1024], P('head', ('grp', 'row'), None, 'sub'), parts along dimension 1, may hold values from -6 to 6
- attn_out: bfloat16 [4, 96, 32, 1024], P('head', ('grp', 'row')), parts along dimension 1, may hold values from -1.796875 to 1.796875
- out_grad: bfloat16 [4, 96, 32, 1024], P('head', ('grp', 'row')), parts along dimension 1, may hold values from -24 to 24
- log_norm: float32 [4, 96, 1024], P('head', ('grp', 'row')), parts along dimension 1, may hold values from 7 to 9
- pair_bias: bfloat16 [8, 1024, 1024], P(('grp', 'head'), 'row', 'sub'), parts along dimension 0, may hold values from -6 to 6
- chain_ids: int32 [2048], P('grp'), parts along dimension 0, may hold values from 0 to 7, as said below
- pair_table: int32 [16, 8], P('grp'), parts along dimension 0, may hold values from 0 to 1, as said below
Outputs:
- query_grad: bfloat16 [4, 96, 32, 1024], P('head', ('grp', 'row'), None, 'sub'), parts along dimension 1
- key_grad: bfloat16 [4, 96, 32, 1024], P('head', ('grp', 'row'), None, 'sub'), parts along dimension 1
- value_grad: bfloat16 [4, 96, 32, 1024], P('head', ('grp', 'row'), None, 'sub'), parts along dimension 1
- bias_grad: float32 [8, 1024, 1024], P(('grp', 'head'), 'row', 'sub'), parts along dimension 0
There are 2 independent parts, one for each index of `grp`. A program takes and returns all parts, laid end to end along the dimension named above; each array names one. Nothing has to cross between parts.
Inputs may be any that keep to these rules, and one draw needn't show every extreme that they name: `chain_ids`: chains are contiguous runs of residues, numbered in order from 0; each of the 8 chains holds at least one residue. `pair_table`: entries are 0 or 1 and the diagonal is 1.
All inputs are finite; a program needn't handle non-finite values.
Results may differ from a plain program's by a relative error of at most 0.0059.
Values may be sent and summed in bfloat16 or wider, within the bound.
A program may use at most 128 MiB of HBM per device.

v0:
```python
import jax
import jax.numpy as jnp
from jax import lax
from jax.sharding import PartitionSpec as P


def score_parts(
    row_query, row_key, row_value, row_grad, row_norm, row_delta, bias_cols, allowed, factor
):
    scores = factor * jnp.einsum(
        "rdj,rdk->rjk", row_query, row_key, preferred_element_type=jnp.float32
    )
    scores = scores + bias_cols.astype(jnp.float32)[None]
    attn_prob = jnp.where(
        allowed[:, None, :], jnp.exp(scores - row_norm[:, :, None]), jnp.zeros_like(scores)
    )
    prob_grad = jnp.einsum("rdj,rdk->rjk", row_grad, row_value, preferred_element_type=jnp.float32)
    score_grad = attn_prob * (prob_grad - row_delta[:, :, None])
    return (attn_prob, score_grad)


def block_terms(
    row_query, row_key, row_value, row_grad, row_norm, row_delta, bias_cols, allowed, factor
):
    attn_prob, score_grad = score_parts(
        row_query, row_key, row_value, row_grad, row_norm, row_delta, bias_cols, allowed, factor
    )
    prob_low = attn_prob.astype(jnp.bfloat16)
    value_part = jnp.einsum("rdj,rjk->rdk", row_grad, prob_low, preferred_element_type=jnp.float32)
    score_low = score_grad.astype(jnp.bfloat16)
    query_part = factor * jnp.einsum(
        "rdk,rjk->rdj", row_key, score_low, preferred_element_type=jnp.float32
    )
    key_part = factor * jnp.einsum(
        "rdj,rjk->rdk", row_query, score_low, preferred_element_type=jnp.float32
    )
    return (query_part, key_part, value_part, jnp.sum(score_grad, axis=0))


def head_work(
    queries, key_side, value_side, attn_out, out_grad, log_norm, bias_full, chain_ids, pair_table
):
    rows_dev = queries.shape[1]
    head_dim = queries.shape[2]
    length = queries.shape[3]
    keys_dev = key_side.shape[3]
    factor = head_dim ** (-0.5)
    row_index = lax.axis_index("row")
    key_first = lax.axis_index("sub") * keys_dev
    key_chain = lax.dynamic_slice_in_dim(chain_ids, key_first, keys_dev)
    labels = jnp.arange(pair_table.shape[0], dtype=jnp.int32)
    key_onehot = (labels[:, None] == key_chain[None, :]).astype(jnp.float32)
    table_float = pair_table.astype(jnp.float32)
    row_chain = lax.dynamic_slice_in_dim(chain_ids, row_index * rows_dev, rows_dev)
    row_onehot = (row_chain[:, None] == labels[None, :]).astype(jnp.float32)
    allowed_all = jnp.dot(jnp.dot(row_onehot, table_float), key_onehot) > 0.5
    delta_all = jnp.sum(out_grad[0].astype(jnp.float32) * attn_out[0].astype(jnp.float32), axis=1)

    def regroup(array):
        return array.reshape((array.shape[0] // 2, 2) + array.shape[1:])

    def grads_for(row_query, row_key, row_value, row_grad, row_norm, row_delta, allowed):
        return block_terms(
            row_query, row_key, row_value, row_grad, row_norm, row_delta, bias_full, allowed, factor
        )

    own_blocks = (
        regroup(queries[0]),
        regroup(key_side[0]),
        regroup(value_side[0]),
        regroup(out_grad[0]),
        regroup(log_norm[0]),
        regroup(delta_all),
        regroup(allowed_all),
    )
    start_sum = jnp.zeros((length, keys_dev), jnp.float32)

    def step(carry, item):
        row_block, flag = item
        parts = grads_for(*row_block)
        query_part, key_part, value_part, bias_part = parts
        updated = carry + bias_part
        return (updated, (query_part, key_part, value_part))

    marks = jnp.ones((own_blocks[0].shape[0],), jnp.bool_)
    running, own_parts = lax.scan(step, start_sum, (own_blocks, marks))
    query_parts, key_parts, value_parts = own_parts
    query_share = query_parts.reshape((1, rows_dev, head_dim, length))
    key_grad = key_parts.reshape((1, rows_dev, head_dim, keys_dev)).astype(jnp.bfloat16)
    value_grad = value_parts.reshape((1, rows_dev, head_dim, keys_dev)).astype(jnp.bfloat16)
    query_grad = lax.psum_scatter(query_share, "sub", scatter_dimension=3, tiled=True).astype(
        jnp.bfloat16
    )
    bias_grad = lax.psum_scatter(running[None], "row", scatter_dimension=1, tiled=True)
    return (query_grad, key_grad, value_grad, bias_grad)


def per_device(
    queries, key_side, value_side, attn_out, out_grad, log_norm, pair_bias, chain_ids, pair_table
):
    bias_all = lax.all_gather(pair_bias, "row", axis=1, tiled=True)
    head_count = queries.shape[0]
    results = []
    for head in range(head_count):
        results.append(
            head_work(
                queries[head : head + 1],
                key_side[head : head + 1],
                value_side[head : head + 1],
                attn_out[head : head + 1],
                out_grad[head : head + 1],
                log_norm[head : head + 1],
                bias_all[head],
                chain_ids,
                pair_table,
            )
        )
    query_grad = jnp.concatenate([item[0] for item in results], axis=0)
    key_grad = jnp.concatenate([item[1] for item in results], axis=0)
    value_grad = jnp.concatenate([item[2] for item in results], axis=0)
    bias_grad = jnp.concatenate([item[3] for item in results], axis=0)
    return (query_grad, key_grad, value_grad, bias_grad)


def solution(mesh):
    return jax.shard_map(
        per_device,
        mesh=mesh,
        in_specs=(
            P("head", ("grp", "row"), None, None),
            P("head", ("grp", "row"), None, "sub"),
            P("head", ("grp", "row"), None, "sub"),
            P("head", ("grp", "row"), None, None),
            P("head", ("grp", "row"), None, None),
            P("head", ("grp", "row"), None),
            P(("grp", "head"), "row", "sub"),
            P("grp"),
            P("grp", None),
        ),
        out_specs=(
            P("head", ("grp", "row"), None, "sub"),
            P("head", ("grp", "row"), None, "sub"),
            P("head", ("grp", "row"), None, "sub"),
            P(("grp", "head"), "row", "sub"),
        ),
        check_vma=False,
    )
```

profile of v0, /device:TPU:12, one launch (start us, length us, event | category | flops | bytes accessed | tf_op | source)
XLA Modules:
  0.0 415.5 jit_solution(13106444879622825534)
XLA Ops:
  13.1 2.6 multiply_reduce_fusion.1
  18.4 2.2 fusion.87
  23.3 31.8 %all-gather.2.cloned.1.call-done = bf16[2,1024,512]{2,1,0:T(8,128)(2,1)} async-done(((bf16[2,256,512]{2,1,0:T(8,128)(2,1)}), bf16[2,1024,512]{2,1,0:T(8,128)(2,1)}) %all-gather.2.cloned.1.call-update) | async-done | bytes 2097168 | tf_op jit(solution)/shard_map/all_gather | solution.py:101
  55.1 2.6 slice_bitcast_fusion.1
  60.6 128.2 %while.35 = (s32[]{:T(128)}, f32[1024,512]{1,0:T(8,128)}, f32[6,2,32,1024]{3,2,1,0:T(8,128)}, bf16[6,2,32,512]{3,2,1,0:T(8,128)(2,1)}, bf16[6,2,32,512]{3,2,1,0:...) while((s32[]{:T(128)}, f32[1024,512]{1,0:T(8,128)}, ...), condition=%wide.region_8.9_spmd.clone, body=%wide.region_6.8_spmd.clone.sunk | while | flops 350322688 | bytes 77858040 | solution.py:86
  65.2 5.7 %fusion.141 = (f32[1024,512]{1,0:T(8,128)}, bf16[2,1024,512]{2,1,0:T(8,128)(2,1)}) fusion(f32[2,1024]{1,0:T(2,128)S(1)} %get-tuple-element.486, bf16[6,2,32,512]{3,2,1,0:T(8,128)(2,1)} %get-tuple-element.531, s32[]{:T(128)S(6)} %copy.26, bf16[6,2,32,1024]{3,2,1,0:T(8,128)(2,1)} %get-tuple-element.530, f32[2,1024]{1,0:T(2,128)S(1)} %get-tuple-element.487, ...), kind=kOutput, calls=%fused_computation.100.clone.1 | convolution fusion | flops 74973184 | bytes 10700800 | tf_op jit(solution)/shard_map/while/body/eval_jaxpr/rdj,rdk->rjk/dot_general | solution.py:17
  70.9 3.6 select_add_fusion.5
  74.5 2.4 fusion.142
  76.9 2.0 fusion.143
  78.9 2.6 fusion.144
  86.1 5.7 %fusion.141 = (f32[1024,512]{1,0:T(8,128)}, bf16[2,1024,512]{2,1,0:T(8,128)(2,1)}) fusion(f32[2,1024]{1,0:T(2,128)S(1)} %get-tuple-element.486, bf16[6,2,32,512]{3,2,1,0:T(8,128)(2,1)} %get-tuple-element.531, s32[]{:T(128)S(6)} %copy.26, bf16[6,2,32,1024]{3,2,1,0:T(8,128)(2,1)} %get-tuple-element.530, f32[2,1024]{1,0:T(2,128)S(1)} %get-tuple-element.487, ...), kind=kOutput, calls=%fused_computation.100.clone.1 | convolution fusion | flops 74973184 | bytes 10700800 | tf_op jit(solution)/shard_map/while/body/eval_jaxpr/rdj,rdk->rjk/dot_general | solution.py:17
  91.8 4.2 %select_add_fusion.5 = f32[1024,512]{1,0:T(8,128)} fusion(f32[1024,512]{1,0:T(8,128)} %get-tuple-element.488, f32[1024,512]{1,0:T(8,128)} %get-tuple-element.506, pred[]{:T(512)S(6)} %compare.7), kind=kLoop, calls=%fused_computation.44.clone.1 | loop fusion | flops 1048576 | bytes 6291457 | tf_op jit(solution)/shard_map/while/body/eval_jaxpr/add | solution.py:82
  96.0 2.4 fusion.142
  98.4 2.0 fusion.143
  100.4 2.6 fusion.144
  107.5 5.7 %fusion.141 = (f32[1024,512]{1,0:T(8,128)}, bf16[2,1024,512]{2,1,0:T(8,128)(2,1)}) fusion(f32[2,1024]{1,0:T(2,128)S(1)} %get-tuple-element.486, bf16[6,2,32,512]{3,2,1,0:T(8,128)(2,1)} %get-tuple-element.531, s32[]{:T(128)S(6)} %copy.26, bf16[6,2,32,1024]{3,2,1,0:T(8,128)(2,1)} %get-tuple-element.530, f32[2,1024]{1,0:T(2,128)S(1)} %get-tuple-element.487, ...), kind=kOutput, calls=%fused_computation.100.clone.1 | convolution fusion | flops 74973184 | bytes 10700800 | tf_op jit(solution)/shard_map/while/body/eval_jaxpr/rdj,rdk->rjk/dot_general | solution.py:17
  113.3 4.2 %select_add_fusion.5 = f32[1024,512]{1,0:T(8,128)} fusion(f32[1024,512]{1,0:T(8,128)} %get-tuple-element.488, f32[1024,512]{1,0:T(8,128)} %get-tuple-element.506, pred[]{:T(512)S(6)} %compare.7), kind=kLoop, calls=%fused_computation.44.clone.1 | loop fusion | flops 1048576 | bytes 6291457 | tf_op jit(solution)/shard_map/while/body/eval_jaxpr/add | solution.py:82
  117.5 2.4 fusion.142
  119.9 2.0 fusion.143
  121.9 2.6 fusion.144
  129.0 5.7 %fusion.141 = (f32[1024,512]{1,0:T(8,128)}, bf16[2,1024,512]{2,1,0:T(8,128)(2,1)}) fusion(f32[2,1024]{1,0:T(2,128)S(1)} %get-tuple-element.486, bf16[6,2,32,512]{3,2,1,0:T(8,128)(2,1)} %get-tuple-element.531, s32[]{:T(128)S(6)} %copy.26, bf16[6,2,32,1024]{3,2,1,0:T(8,128)(2,1)} %get-tuple-element.530, f32[2,1024]{1,0:T(2,128)S(1)} %get-tuple-element.487, ...), kind=kOutput, calls=%fused_computation.100.clone.1 | convolution fusion | flops 74973184 | bytes 10700800 | tf_op jit(solution)/shard_map/while/body/eval_jaxpr/rdj,rdk->rjk/dot_general | solution.py:17
  134.7 4.2 %select_add_fusion.5 = f32[1024,512]{1,0:T(8,128)} fusion(f32[1024,512]{1,0:T(8,128)} %get-tuple-element.488, f32[1024,512]{1,0:T(8,128)} %get-tuple-element.506, pred[]{:T(512)S(6)} %compare.7), kind=kLoop, calls=%fused_computation.44.clone.1 | loop fusion | flops 1048576 | bytes 6291457 | tf_op jit(solution)/shard_map/while/body/eval_jaxpr/add | solution.py:82
  138.9 2.4 fusion.142
  141.3 2.0 fusion.143
  143.3 2.6 fusion.144
  150.5 5.7 %fusion.141 = (f32[1024,512]{1,0:T(8,128)}, bf16[2,1024,512]{2,1,0:T(8,128)(2,1)}) fusion(f32[2,1024]{1,0:T(2,128)S(1)} %get-tuple-element.486, bf16[6,2,32,512]{3,2,1,0:T(8,128)(2,1)} %get-tuple-element.531, s32[]{:T(128)S(6)} %copy.26, bf16[6,2,32,1024]{3,2,1,0:T(8,128)(2,1)} %get-tuple-element.530, f32[2,1024]{1,0:T(2,128)S(1)} %get-tuple-element.487, ...), kind=kOutput, calls=%fused_computation.100.clone.1 | convolution fusion | flops 74973184 | bytes 10700800 | tf_op jit(solution)/shard_map/while/body/eval_jaxpr/rdj,rdk->rjk/dot_general | solution.py:17
  156.2 4.2 %select_add_fusion.5 = f32[1024,512]{1,0:T(8,128)} fusion(f32[1024,512]{1,0:T(8,128)} %get-tuple-element.488, f32[1024,512]{1,0:T(8,128)} %get-tuple-element.506, pred[]{:T(512)S(6)} %compare.7), kind=kLoop, calls=%fused_computation.44.clone.1 | loop fusion | flops 1048576 | bytes 6291457 | tf_op jit(solution)/shard_map/while/body/eval_jaxpr/add | solution.py:82
  160.4 2.4 fusion.142
  162.8 2.0 fusion.143
  164.8 2.6 fusion.144
  171.9 5.7 %fusion.141 = (f32[1024,512]{1,0:T(8,128)}, bf16[2,1024,512]{2,1,0:T(8,128)(2,1)}) fusion(f32[2,1024]{1,0:T(2,128)S(1)} %get-tuple-element.486, bf16[6,2,32,512]{3,2,1,0:T(8,128)(2,1)} %get-tuple-element.531, s32[]{:T(128)S(6)} %copy.26, bf16[6,2,32,1024]{3,2,1,0:T(8,128)(2,1)} %get-tuple-element.530, f32[2,1024]{1,0:T(2,128)S(1)} %get-tuple-element.487, ...), kind=kOutput, calls=%fused_computation.100.clone.1 | convolution fusion | flops 74973184 | bytes 10700800 | tf_op jit(solution)/shard_map/while/body/eval_jaxpr/rdj,rdk->rjk/dot_general | solution.py:17
  177.7 4.2 %select_add_fusion.5 = f32[1024,512]{1,0:T(8,128)} fusion(f32[1024,512]{1,0:T(8,128)} %get-tuple-element.488, f32[1024,512]{1,0:T(8,128)} %get-tuple-element.506, pred[]{:T(512)S(6)} %compare.7), kind=kLoop, calls=%fused_computation.44.clone.1 | loop fusion | flops 1048576 | bytes 6291457 | tf_op jit(solution)/shard_map/while/body/eval_jaxpr/add | solution.py:82
  181.9 2.4 fusion.142
  184.3 2.0 fusion.143
  186.3 2.6 fusion.144
  191.8 114.9 %while.34 = (s32[]{:T(128)}, f32[1024,512]{1,0:T(8,128)}, f32[6,2,32,1024]{3,2,1,0:T(8,128)}, bf16[6,2,32,512]{3,2,1,0:T(8,128)(2,1)}, bf16[6,2,32,512]{3,2,1,0:...) while((s32[]{:T(128)}, f32[1024,512]{1,0:T(8,128)}, ...), condition=%wide.region_3.4_spmd.clone, body=%wide.region_1.3_spmd.clone.sunk | while | flops 350322688 | bytes 77858040 | solution.py:86
  195.2 5.8 %fusion.128 = (f32[1024,512]{1,0:T(8,128)}, bf16[2,1024,512]{2,1,0:T(8,128)(2,1)}) fusion(f32[2,1024]{1,0:T(2,128)S(1)} %get-tuple-element.469, bf16[6,2,32,512]{3,2,1,0:T(8,128)(2,1)} %get-tuple-element.576, s32[]{:T(128)S(6)} %copy.41, bf16[6,2,32,1024]{3,2,1,0:T(8,128)(2,1)} %get-tuple-element.575, f32[2,1024]{1,0:T(2,128)S(1)} %get-tuple-element.470, ...), kind=kOutput, calls=%fused_computation.99.clone.1 | convolution fusion | flops 74973184 | bytes 10700800 | tf_op jit(solution)/shard_map/while/body/eval_jaxpr/rdj,rdk->rjk/dot_general | solution.py:17
  200.9 3.6 select_add_fusion.4
  205.9 2.0 fusion.130
  207.9 2.6 fusion.131
  213.8 5.7 %fusion.128 = (f32[1024,512]{1,0:T(8,128)}, bf16[2,1024,512]{2,1,0:T(8,128)(2,1)}) fusion(f32[2,1024]{1,0:T(2,128)S(1)} %get-tuple-element.469, bf16[6,2,32,512]{3,2,1,0:T(8,128)(2,1)} %get-tuple-element.576, s32[]{:T(128)S(6)} %copy.41, bf16[6,2,32,1024]{3,2,1,0:T(8,128)(2,1)} %get-tuple-element.575, f32[2,1024]{1,0:T(2,128)S(1)} %get-tuple-element.470, ...), kind=kOutput, calls=%fused_computation.99.clone.1 | convolution fusion | flops 74973184 | bytes 10700800 | tf_op jit(solution)/shard_map/while/body/eval_jaxpr/rdj,rdk->rjk/dot_general | solution.py:17
  219.5 4.2 %select_add_fusion.4 = f32[1024,512]{1,0:T(8,128)} fusion(f32[1024,512]{1,0:T(8,128)} %get-tuple-element.471, f32[1024,512]{1,0:T(8,128)} %get-tuple-element.551, pred[]{:T(512)S(6)} %compare.6), kind=kLoop, calls=%fused_computation.3.clone.1 | loop fusion | flops 1048576 | bytes 6291457 | tf_op jit(solution)/shard_map/while/body/eval_jaxpr/add | solution.py:82
  225.2 2.0 fusion.130
  227.1 2.6 fusion.131
  233.1 5.7 %fusion.128 = (f32[1024,512]{1,0:T(8,128)}, bf16[2,1024,512]{2,1,0:T(8,128)(2,1)}) fusion(f32[2,1024]{1,0:T(2,128)S(1)} %get-tuple-element.469, bf16[6,2,32,512]{3,2,1,0:T(8,128)(2,1)} %get-tuple-element.576, s32[]{:T(128)S(6)} %copy.41, bf16[6,2,32,1024]{3,2,1,0:T(8,128)(2,1)} %get-tuple-element.575, f32[2,1024]{1,0:T(2,128)S(1)} %get-tuple-element.470, ...), kind=kOutput, calls=%fused_computation.99.clone.1 | convolution fusion | flops 74973184 | bytes 10700800 | tf_op jit(solution)/shard_map/while/body/eval_jaxpr/rdj,rdk->rjk/dot_general | solution.py:17
  238.8 4.2 %select_add_fusion.4 = f32[1024,512]{1,0:T(8,128)} fusion(f32[1024,512]{1,0:T(8,128)} %get-tuple-element.471, f32[1024,512]{1,0:T(8,128)} %get-tuple-element.551, pred[]{:T(512)S(6)} %compare.6), kind=kLoop, calls=%fused_computation.3.clone.1 | loop fusion | flops 1048576 | bytes 6291457 | tf_op jit(solution)/shard_map/while/body/eval_jaxpr/add | solution.py:82
  244.4 2.0 fusion.130
  246.4 2.6 fusion.131
  252.3 5.7 %fusion.128 = (f32[1024,512]{1,0:T(8,128)}, bf16[2,1024,512]{2,1,0:T(8,128)(2,1)}) fusion(f32[2,1024]{1,0:T(2,128)S(1)} %get-tuple-element.469, bf16[6,2,32,512]{3,2,1,0:T(8,128)(2,1)} %get-tuple-element.576, s32[]{:T(128)S(6)} %copy.41, bf16[6,2,32,1024]{3,2,1,0:T(8,128)(2,1)} %get-tuple-element.575, f32[2,1024]{1,0:T(2,128)S(1)} %get-tuple-element.470, ...), kind=kOutput, calls=%fused_computation.99.clone.1 | convolution fusion | flops 74973184 | bytes 10700800 | tf_op jit(solution)/shard_map/while/body/eval_jaxpr/rdj,rdk->rjk/dot_general | solution.py:17
  258.1 4.2 %select_add_fusion.4 = f32[1024,512]{1,0:T(8,128)} fusion(f32[1024,512]{1,0:T(8,128)} %get-tuple-element.471, f32[1024,512]{1,0:T(8,128)} %get-tuple-element.551, pred[]{:T(512)S(6)} %compare.6), kind=kLoop, calls=%fused_computation.3.clone.1 | loop fusion | flops 1048576 | bytes 6291457 | tf_op jit(solution)/shard_map/while/body/eval_jaxpr/add | solution.py:82
  263.7 2.0 fusion.130
  265.7 2.6 fusion.131
  271.6 5.7 %fusion.128 = (f32[1024,512]{1,0:T(8,128)}, bf16[2,1024,512]{2,1,0:T(8,128)(2,1)}) fusion(f32[2,1024]{1,0:T(2,128)S(1)} %get-tuple-element.469, bf16[6,2,32,512]{3,2,1,0:T(8,128)(2,1)} %get-tuple-element.576, s32[]{:T(128)S(6)} %copy.41, bf16[6,2,32,1024]{3,2,1,0:T(8,128)(2,1)} %get-tuple-element.575, f32[2,1024]{1,0:T(2,128)S(1)} %get-tuple-element.470, ...), kind=kOutput, calls=%fused_computation.99.clone.1 | convolution fusion | flops 74973184 | bytes 10700800 | tf_op jit(solution)/shard_map/while/body/eval_jaxpr/rdj,rdk->rjk/dot_general | solution.py:17
  277.3 4.2 %select_add_fusion.4 = f32[1024,512]{1,0:T(8,128)} fusion(f32[1024,512]{1,0:T(8,128)} %get-tuple-element.471, f32[1024,512]{1,0:T(8,128)} %get-tuple-element.551, pred[]{:T(512)S(6)} %compare.6), kind=kLoop, calls=%fused_computation.3.clone.1 | loop fusion | flops 1048576 | bytes 6291457 | tf_op jit(solution)/shard_map/while/body/eval_jaxpr/add | solution.py:82
  282.9 2.0 fusion.130
  284.9 2.6 fusion.131
  290.8 5.7 %fusion.128 = (f32[1024,512]{1,0:T(8,128)}, bf16[2,1024,512]{2,1,0:T(8,128)(2,1)}) fusion(f32[2,1024]{1,0:T(2,128)S(1)} %get-tuple-element.469, bf16[6,2,32,512]{3,2,1,0:T(8,128)(2,1)} %get-tuple-element.576, s32[]{:T(128)S(6)} %copy.41, bf16[6,2,32,1024]{3,2,1,0:T(8,128)(2,1)} %get-tuple-element.575, f32[2,1024]{1,0:T(2,128)S(1)} %get-tuple-element.470, ...), kind=kOutput, calls=%fused_computation.99.clone.1 | convolution fusion | flops 74973184 | bytes 10700800 | tf_op jit(solution)/shard_map/while/body/eval_jaxpr/rdj,rdk->rjk/dot_general | solution.py:17
  296.5 4.2 %select_add_fusion.4 = f32[1024,512]{1,0:T(8,128)} fusion(f32[1024,512]{1,0:T(8,128)} %get-tuple-element.471, f32[1024,512]{1,0:T(8,128)} %get-tuple-element.551, pred[]{:T(512)S(6)} %compare.6), kind=kLoop, calls=%fused_computation.3.clone.1 | loop fusion | flops 1048576 | bytes 6291457 | tf_op jit(solution)/shard_map/while/body/eval_jaxpr/add | solution.py:82
  302.2 2.0 fusion.130
  304.2 2.6 fusion.131
  310.6 6.0 %reduce-scatter.5.cloned.1.call-done = f32[1,12,32,512]{3,2,1,0:T(8,128)} async-done(((f32[1,12,32,1024]{3,2,1,0:T(8,128)}), f32[1,12,32,512]{3,2,1,0:T(8,128)}) %reduce-scatter.5.cloned.1.call-update) | async-done | bytes 786448 | tf_op jit(solution)/shard_map/reduce_scatter | solution.py:91
  318.7 42.6 %reduce-scatter.11.cloned.1.call-done = f32[1,256,512]{2,1,0:T(8,128)} async-done(((f32[1,1024,512]{2,1,0:T(8,128)}), f32[1,256,512]{2,1,0:T(8,128)}) %reduce-scatter.11.cloned.1.call-update) | async-done | bytes 524304 | tf_op jit(solution)/shard_map/reduce_scatter | solution.py:94
  361.3 45.4 %reduce-scatter.9.cloned.1.call-done = f32[1,256,512]{2,1,0:T(8,128)} async-done(((f32[1,1024,512]{2,1,0:T(8,128)}), f32[1,256,512]{2,1,0:T(8,128)}) %reduce-scatter.9.cloned.1.call-update) | async-done | bytes 524304 | tf_op jit(solution)/shard_map/reduce_scatter | solution.py:94
  406.8 2.2 pad_maximum_fusion
  (175 shorter events, 79.1 us)
Async XLA Ops:
  7.2 47.9 %all-gather.2.cloned.1.call-start = ((), (), s32[]{:S(2)}) async-start(), calls=%async_computation.4 | async-start | bytes 2621440 | tf_op jit(solution)/shard_map/all_gather | solution.py:101
  7.9 9.7 %copy-start.12 = (bf16[2,12,32,512]{3,2,1,0:T(8,128)(2,1)S(1)}, bf16[2,12,32,512]{3,2,1,0:T(8,128)(2,1)}, u32[]{:S(2)}) copy-start(bf16[2,12,32,512]{3,2,1,0:T(8,128)(2,1)} %param.14) | copy-start | bytes 2359300
  7.9 301.5 %reduce-scatter.7.cloned.1.call-start = ((), (), s32[]{:S(2)}) async-start(), calls=%async_computation.6 | async-start | bytes 2359296 | tf_op jit(solution)/shard_map/reduce_scatter | solution.py:91
  15.7 5.0 %copy-start.6 = (bf16[2,12,32,1024]{3,2,1,0:T(8,128)(2,1)S(1)}, bf16[2,12,32,1024]{3,2,1,0:T(8,128)(2,1)}, u32[]{:S(2)}) copy-start(bf16[2,12,32,1024]{3,2,1,0:T(8,128)(2,1)} %param.17) | copy-start | bytes 4718596
  18.4 3.6 copy-start.7
  64.5 6.4 %copy-start = (f32[2,1024,512]{2,1,0:T(8,128)}, f32[2,1024,512]{2,1,0:T(8,128)S(1)}, u32[]{:S(2)}) copy-start(f32[2,1024,512]{2,1,0:T(8,128)S(1)} %fusion.140) | copy-start | bytes 12582916 | tf_op jit(solution)/shard_map/while
  70.9 3.6 copy-start.4
  74.5 4.4 %copy-start.1 = (f32[2,1024,512]{2,1,0:T(8,128)S(1)}, f32[2,1024,512]{2,1,0:T(8,128)}, u32[]{:S(2)}) copy-start(f32[2,1024,512]{2,1,0:T(8,128)} %copy-done) | copy-start | bytes 12582916 | tf_op jit(solution)/shard_map/while
  85.4 6.4 %copy-start = (f32[2,1024,512]{2,1,0:T(8,128)}, f32[2,1024,512]{2,1,0:T(8,128)S(1)}, u32[]{:S(2)}) copy-start(f32[2,1024,512]{2,1,0:T(8,128)S(1)} %fusion.140) | copy-start | bytes 12582916 | tf_op jit(solution)/shard_map/while
  91.8 4.2 %copy-start.4 = (bf16[2,1024,512]{2,1,0:T(8,128)(2,1)S(1)}, bf16[2,1024,512]{2,1,0:T(8,128)(2,1)}, u32[]{:S(2)}) copy-start(bf16[2,1024,512]{2,1,0:T(8,128)(2,1)} %get-tuple-element.489) | copy-start | bytes 6291460 | tf_op jit(solution)/shard_map/while
  96.0 4.4 %copy-start.1 = (f32[2,1024,512]{2,1,0:T(8,128)S(1)}, f32[2,1024,512]{2,1,0:T(8,128)}, u32[]{:S(2)}) copy-start(f32[2,1024,512]{2,1,0:T(8,128)} %copy-done) | copy-start | bytes 12582916 | tf_op jit(solution)/shard_map/while
  106.8 6.4 %copy-start = (f32[2,1024,512]{2,1,0:T(8,128)}, f32[2,1024,512]{2,1,0:T(8,128)S(1)}, u32[]{:S(2)}) copy-start(f32[2,1024,512]{2,1,0:T(8,128)S(1)} %fusion.140) | copy-start | bytes 12582916 | tf_op jit(solution)/shard_map/while
  113.2 4.2 %copy-start.4 = (bf16[2,1024,512]{2,1,0:T(8,128)(2,1)S(1)}, bf16[2,1024,512]{2,1,0:T(8,128)(2,1)}, u32[]{:S(2)}) copy-start(bf16[2,1024,512]{2,1,0:T(8,128)(2,1)} %get-tuple-element.489) | copy-start | bytes 6291460 | tf_op jit(solution)/shard_map/while
  117.5 4.4 %copy-start.1 = (f32[2,1024,512]{2,1,0:T(8,128)S(1)}, f32[2,1024,512]{2,1,0:T(8,128)}, u32[]{:S(2)}) copy-start(f32[2,1024,512]{2,1,0:T(8,128)} %copy-done) | copy-start | bytes 12582916 | tf_op jit(solution)/shard_map/while
  128.3 6.4 %copy-start = (f32[2,1024,512]{2,1,0:T(8,128)}, f32[2,1024,512]{2,1,0:T(8,128)S(1)}, u32[]{:S(2)}) copy-start(f32[2,1024,512]{2,1,0:T(8,128)S(1)} %fusion.140) | copy-start | bytes 12582916 | tf_op jit(solution)/shard_map/while
  134.7 4.2 %copy-start.4 = (bf16[2,1024,512]{2,1,0:T(8,128)(2,1)S(1)}, bf16[2,1024,512]{2,1,0:T(8,128)(2,1)}, u32[]{:S(2)}) copy-start(bf16[2,1024,512]{2,1,0:T(8,128)(2,1)} %get-tuple-element.489) | copy-start | bytes 6291460 | tf_op jit(solution)/shard_map/while
  138.9 4.4 %copy-start.1 = (f32[2,1024,512]{2,1,0:T(8,128)S(1)}, f32[2,1024,512]{2,1,0:T(8,128)}, u32[]{:S(2)}) copy-start(f32[2,1024,512]{2,1,0:T(8,128)} %copy-done) | copy-start | bytes 12582916 | tf_op jit(solution)/shard_map/while
  149.8 6.4 %copy-start = (f32[2,1024,512]{2,1,0:T(8,128)}, f32[2,1024,512]{2,1,0:T(8,128)S(1)}, u32[]{:S(2)}) copy-start(f32[2,1024,512]{2,1,0:T(8,128)S(1)} %fusion.140) | copy-start | bytes 12582916 | tf_op jit(solution)/shard_map/while
  156.2 4.2 %copy-start.4 = (bf16[2,1024,512]{2,1,0:T(8,128)(2,1)S(1)}, bf16[2,1024,512]{2,1,0:T(8,128)(2,1)}, u32[]{:S(2)}) copy-start(bf16[2,1024,512]{2,1,0:T(8,128)(2,1)} %get-tuple-element.489) | copy-start | bytes 6291460 | tf_op jit(solution)/shard_map/while
  160.4 4.4 %copy-start.1 = (f32[2,1024,512]{2,1,0:T(8,128)S(1)}, f32[2,1024,512]{2,1,0:T(8,128)}, u32[]{:S(2)}) copy-start(f32[2,1024,512]{2,1,0:T(8,128)} %copy-done) | copy-start | bytes 12582916 | tf_op jit(solution)/shard_map/while
  171.3 6.4 %copy-start = (f32[2,1024,512]{2,1,0:T(8,128)}, f32[2,1024,512]{2,1,0:T(8,128)S(1)}, u32[]{:S(2)}) copy-start(f32[2,1024,512]{2,1,0:T(8,128)S(1)} %fusion.140) | copy-start | bytes 12582916 | tf_op jit(solution)/shard_map/while
  177.7 4.2 %copy-start.4 = (bf16[2,1024,512]{2,1,0:T(8,128)(2,1)S(1)}, bf16[2,1024,512]{2,1,0:T(8,128)(2,1)}, u32[]{:S(2)}) copy-start(bf16[2,1024,512]{2,1,0:T(8,128)(2,1)} %get-tuple-element.489) | copy-start | bytes 6291460 | tf_op jit(solution)/shard_map/while
  181.9 4.4 %copy-start.1 = (f32[2,1024,512]{2,1,0:T(8,128)S(1)}, f32[2,1024,512]{2,1,0:T(8,128)}, u32[]{:S(2)}) copy-start(f32[2,1024,512]{2,1,0:T(8,128)} %copy-done) | copy-start | bytes 12582916 | tf_op jit(solution)/shard_map/while
  188.8 127.8 %reduce-scatter.5.cloned.1.call-start = ((), (), s32[]{:S(2)}) async-start(), calls=%async_computation.5 | async-start | bytes 2359296 | tf_op jit(solution)/shard_map/reduce_scatter | solution.py:91
  194.5 6.4 %copy-start.2 = (f32[2,1024,512]{2,1,0:T(8,128)}, f32[2,1024,512]{2,1,0:T(8,128)S(1)}, u32[]{:S(2)}) copy-start(f32[2,1024,512]{2,1,0:T(8,128)S(1)} %fusion.127) | copy-start | bytes 12582916 | tf_op jit(solution)/shard_map/while
  200.9 3.6 copy-start.5
  204.5 3.4 copy-start.3
  213.1 6.4 %copy-start.2 = (f32[2,1024,512]{2,1,0:T(8,128)}, f32[2,1024,512]{2,1,0:T(8,128)S(1)}, u32[]{:S(2)}) copy-start(f32[2,1024,512]{2,1,0:T(8,128)S(1)} %fusion.127) | copy-start | bytes 12582916 | tf_op jit(solution)/shard_map/while
  219.5 4.2 %copy-start.5 = (bf16[2,1024,512]{2,1,0:T(8,128)(2,1)S(1)}, bf16[2,1024,512]{2,1,0:T(8,128)(2,1)}, u32[]{:S(2)}) copy-start(bf16[2,1024,512]{2,1,0:T(8,128)(2,1)} %get-tuple-element.472) | copy-start | bytes 6291460 | tf_op jit(solution)/shard_map/while
  223.7 3.4 copy-start.3
  232.4 6.4 %copy-start.2 = (f32[2,1024,512]{2,1,0:T(8,128)}, f32[2,1024,512]{2,1,0:T(8,128)S(1)}, u32[]{:S(2)}) copy-start(f32[2,1024,512]{2,1,0:T(8,128)S(1)} %fusion.127) | copy-start | bytes 12582916 | tf_op jit(solution)/shard_map/while
  238.8 4.2 %copy-start.5 = (bf16[2,1024,512]{2,1,0:T(8,128)(2,1)S(1)}, bf16[2,1024,512]{2,1,0:T(8,128)(2,1)}, u32[]{:S(2)}) copy-start(bf16[2,1024,512]{2,1,0:T(8,128)(2,1)} %get-tuple-element.472) | copy-start | bytes 6291460 | tf_op jit(solution)/shard_map/while
  243.0 3.4 copy-start.3
  251.6 6.4 %copy-start.2 = (f32[2,1024,512]{2,1,0:T(8,128)}, f32[2,1024,512]{2,1,0:T(8,128)S(1)}, u32[]{:S(2)}) copy-start(f32[2,1024,512]{2,1,0:T(8,128)S(1)} %fusion.127) | copy-start | bytes 12582916 | tf_op jit(solution)/shard_map/while
  258.1 4.2 %copy-start.5 = (bf16[2,1024,512]{2,1,0:T(8,128)(2,1)S(1)}, bf16[2,1024,512]{2,1,0:T(8,128)(2,1)}, u32[]{:S(2)}) copy-start(bf16[2,1024,512]{2,1,0:T(8,128)(2,1)} %get-tuple-element.472) | copy-start | bytes 6291460 | tf_op jit(solution)/shard_map/while
  262.2 3.4 copy-start.3
  270.9 6.4 %copy-start.2 = (f32[2,1024,512]{2,1,0:T(8,128)}, f32[2,1024,512]{2,1,0:T(8,128)S(1)}, u32[]{:S(2)}) copy-start(f32[2,1024,512]{2,1,0:T(8,128)S(1)} %fusion.127) | copy-start | bytes 12582916 | tf_op jit(solution)/shard_map/while
  277.3 4.2 %copy-start.5 = (bf16[2,1024,512]{2,1,0:T(8,128)(2,1)S(1)}, bf16[2,1024,512]{2,1,0:T(8,128)(2,1)}, u32[]{:S(2)}) copy-start(bf16[2,1024,512]{2,1,0:T(8,128)(2,1)} %get-tuple-element.472) | copy-start | bytes 6291460 | tf_op jit(solution)/shard_map/while
  281.5 3.4 copy-start.3
  290.2 6.4 %copy-start.2 = (f32[2,1024,512]{2,1,0:T(8,128)}, f32[2,1024,512]{2,1,0:T(8,128)S(1)}, u32[]{:S(2)}) copy-start(f32[2,1024,512]{2,1,0:T(8,128)S(1)} %fusion.127) | copy-start | bytes 12582916 | tf_op jit(solution)/shard_map/while
  296.5 4.2 %copy-start.5 = (bf16[2,1024,512]{2,1,0:T(8,128)(2,1)S(1)}, bf16[2,1024,512]{2,1,0:T(8,128)(2,1)}, u32[]{:S(2)}) copy-start(bf16[2,1024,512]{2,1,0:T(8,128)(2,1)} %get-tuple-element.472) | copy-start | bytes 6291460 | tf_op jit(solution)/shard_map/while
  300.7 3.4 copy-start.3
  306.8 54.5 %reduce-scatter.11.cloned.1.call-start = ((), (), s32[]{:S(2)}) async-start(), calls=%async_computation.8 | async-start | bytes 2621440 | tf_op jit(solution)/shard_map/reduce_scatter | solution.py:94
  306.8 1.1 copy-start.8
  306.8 1.1 copy-start.9
  306.8 1.2 copy-start.10
  306.8 1.3 copy-start.11
  307.3 99.4 %reduce-scatter.9.cloned.1.call-start = ((), (), s32[]{:S(2)}) async-start(), calls=%async_computation.7 | async-start | bytes 2621440 | tf_op jit(solution)/shard_map/reduce_scatter | solution.py:94
Sparse Core Ops, SparseCore 0:
  9.6 45.4 all-gather.1
  189.0 9.6 reduce-scatter.6
  306.9 9.6 reduce-scatter.4
  318.8 42.4 reduce-scatter.10
  363.5 43.1 reduce-scatter.8
where the time goes:
time: 422 us; the launch traced here: 416 us
  matrix products  167 us (40%)
  waiting for transfers between devices  127 us (30%)
  other arithmetic  69.1 us (16%)
  local copies, waits for them, and re-layouts  37.3 us (9%)
  between operations  13.9 us (3%)
    reduce_scatter x2, waiting for transfers between devices, head_work(): lax.psum_scatter(running[None], 'row', scatter_dimension=1, tiled=True)  88 us
    dot_general x12, matrix products, score_parts(): jnp.einsum('rdj,rdk->rjk', row_grad, row_value, preferred_element_type=jn...  68.5 us
    add x12, other arithmetic, step(): updated = carry + bias_part  49 us
    all_gather x1, waiting for transfers between devices, per_device(): bias_all = lax.all_gather(pair_bias, 'row', axis=1, tiled=True)  31.8 us
    dot_general x12, matrix products, block_terms(): jnp.einsum('rdj,rjk->rdk', row_grad, prob_low, preferred_element_type=jnp...  30.8 us
    dot_general x12, matrix products, block_terms(): jnp.einsum('rdj,rjk->rdk', row_query, score_low, preferred_element_type=j...  23.8 us
    dot_general x12, matrix products, block_terms(): jnp.einsum('rdk,rjk->rdj', row_key, score_low, preferred_element_type=jnp...  23.1 us
    dot_general x12, matrix products, score_parts(): jnp.einsum('rdj,rdk->rjk', row_query, row_key, preferred_element_type=jnp...  19.9 us
  transfers between devices with their start and end apart: 5, of which 4 were waited for; matrix products, arithmetic and copies ran while one was open for 33% of the time, Pallas kernels for 0%

commit v1 on v0

v1 whole, which is shorter than its diff:
```python
import functools
import math

import jax
import jax.numpy as jnp
from jax import lax
from jax.experimental import pallas as pl
from jax.experimental.pallas import tpu as pltpu
from jax.sharding import PartitionSpec as P

F32 = jnp.float32
BF16 = jnp.bfloat16
LOG2E = math.log2(math.e)
MASKED = -16384.0


def three_parts(value):
    high = value.astype(BF16).astype(F32)
    rest = value - high
    mid = rest.astype(BF16).astype(F32)
    return high, mid, rest - mid


def prepare_row(h, i, key_first, row_first, refs):
    k_ref, v_ref, o_ref, do_ref, n_ref, ids_ref, chain_ref, table_ref, aug_ref, rhs_ref = refs
    head_dim, length = o_ref.shape[2], o_ref.shape[3]
    keys = k_ref.shape[3]
    delta = jnp.sum(do_ref[h, i].astype(F32) * o_ref[h, i].astype(F32), axis=0, keepdims=True)
    n1, n2, n3 = three_parts(n_ref[h, pl.ds(i, 1), :] * (-LOG2E))
    d1, d2, d3 = three_parts(-delta)
    line = lax.broadcasted_iota(jnp.int32, (head_dim, length), 0)
    aug = jnp.where(line == 3, 1.0, 0.0)
    for at, part in ((0, n1), (1, n2), (2, n3), (4, d1), (5, d2), (6, d3)):
        aug = jnp.where(line == at, part, aug)
    aug_ref[h, i] = aug.astype(BF16)
    key_chain = chain_ref[:, pl.ds(key_first, keys)]
    row_chain = ids_ref[0, row_first + i]
    seen = jnp.zeros((1, keys), jnp.int32)
    for label in range(table_ref.shape[1]):
        seen = jnp.where(key_chain == label, table_ref[row_chain, label], seen)
    shut = jnp.where(seen == 1, 0.0, MASKED)
    scaled = k_ref[h, i].astype(F32) * (head_dim ** -0.5 * LOG2E)
    high = scaled.astype(BF16)
    low = (scaled - high.astype(F32)).astype(BF16)
    line = lax.broadcasted_iota(jnp.int32, (head_dim, keys), 0)
    score_side = jnp.where(line < 3, 1.0, jnp.where(line == 3, shut, 0.0))
    prob_side = jnp.where((line >= 4) & (line < 7), 1.0, 0.0)
    none = jnp.zeros((head_dim, keys), BF16)
    rhs_ref[h, i, :, :keys] = jnp.concatenate([high, low, none, score_side.astype(BF16)], axis=0)
    rhs_ref[h, i, :, keys:] = jnp.concatenate(
        [none, none, v_ref[h, i], prob_side.astype(BF16)], axis=0
    )


def row_step(h, i, columns, refs):
    q_ref, k_ref, do_ref, aug_ref, rhs_ref, bias_ref, acc_ref, dq_ref, dk_ref, dv_ref = refs
    keys = k_ref.shape[3]
    chunk = min(256, keys)
    query = q_ref[h, i, :, columns]
    grad = do_ref[h, i, :, columns]
    left = jnp.concatenate([query, query, grad, aug_ref[h, i, :, columns]], axis=0).T
    dq = None
    for first in range(0, keys, chunk):
        part = pl.ds(first, chunk)
        scores = jnp.dot(left, rhs_ref[h, i, :, part], preferred_element_type=F32)
        prob_grad = jnp.dot(
            left, rhs_ref[h, i, :, pl.ds(keys + first, chunk)], preferred_element_type=F32
        )
        prob = jnp.exp2(scores + bias_ref[:, part])
        score_grad = prob * prob_grad
        acc_ref[:, part] += score_grad
        low = score_grad.astype(BF16)
        dv_ref[i, :, part] += jnp.dot(grad, prob.astype(BF16), preferred_element_type=F32)
        dk_ref[i, :, part] += jnp.dot(query, low, preferred_element_type=F32)
        share = lax.dot_general(
            k_ref[h, i, :, part], low, (((1,), (1,)), ((), ())), preferred_element_type=F32
        )
        dq = share if dq is None else dq + share
    return dq


def local_kernel(
    ids_ref, table_ref, chain_ref, q_ref, k_ref, v_ref, o_ref, do_ref, n_ref, b_ref,
    dq_ref, dk_ref, dv_ref, db_ref, aug_ref, rhs_ref, bias_ref, dk_acc, dv_acc,
):
    heads, rows, head_dim, length = q_ref.shape
    keys = k_ref.shape[3]
    tile = bias_ref.shape[0]
    factor = head_dim ** -0.5
    key_first = pl.multiple_of(lax.axis_index("sub") * keys, keys)
    row_first = lax.axis_index("row") * rows
    prep = (k_ref, v_ref, o_ref, do_ref, n_ref, ids_ref, chain_ref, table_ref, aug_ref, rhs_ref)

    for h in range(heads):
        @pl.loop(0, rows)
        def _(i):
            prepare_row(h, i, key_first, row_first, prep)

    for h in range(heads):
        dk_acc[...] = jnp.zeros_like(dk_acc)
        dv_acc[...] = jnp.zeros_like(dv_acc)

        @pl.loop(0, length // tile)
        def _(block):
            columns = pl.ds(pl.multiple_of(block * tile, tile), tile)
            bias_ref[...] = b_ref[h, columns, :].astype(F32) * LOG2E
            acc_ref = db_ref.at[h, columns, :]
            acc_ref[...] = jnp.zeros_like(acc_ref)
            refs = (
                q_ref, k_ref, do_ref, aug_ref, rhs_ref, bias_ref, acc_ref, dq_ref, dk_acc, dv_acc
            )

            def body(i, carry):
                dq_ref[h, i, :, columns] = factor * row_step(h, i, columns, refs)
                return carry

            lax.fori_loop(0, rows, body, 0, unroll=2 if rows % 2 == 0 else 1)

        dk_ref[h] = (factor * dk_acc[...]).astype(BF16)
        dv_ref[h] = dv_acc[...].astype(BF16)


def per_device(
    queries, key_side, value_side, attn_out, out_grad, log_norm, pair_bias, chain_ids, pair_table
):
    heads, rows, head_dim, length = queries.shape
    keys = key_side.shape[3]
    tile = min(256, length)
    bias_all = lax.all_gather(pair_bias, "row", axis=1, tiled=True)
    vmem = pl.BlockSpec(memory_space=pltpu.VMEM)
    smem = pl.BlockSpec(memory_space=pltpu.SMEM)
    ids = chain_ids.reshape(1, length)
    share, key_grad, value_grad, running = pl.pallas_call(
        local_kernel,
        out_shape=(
            jax.ShapeDtypeStruct((heads, rows, head_dim, length), F32),
            jax.ShapeDtypeStruct((heads, rows, head_dim, keys), BF16),
            jax.ShapeDtypeStruct((heads, rows, head_dim, keys), BF16),
            jax.ShapeDtypeStruct((heads, length, keys), F32),
        ),
        in_specs=[smem, smem] + [vmem] * 8,
        out_specs=(vmem,) * 4,
        scratch_shapes=[
            pltpu.VMEM((heads, rows, head_dim, length), BF16),
            pltpu.VMEM((heads, rows, 4 * head_dim, 2 * keys), BF16),
            pltpu.VMEM((tile, keys), F32),
            pltpu.VMEM((rows, head_dim, keys), F32),
            pltpu.VMEM((rows, head_dim, keys), F32),
        ],
        compiler_params=pltpu.CompilerParams(vmem_limit_bytes=56 * 1024 * 1024),
    )(ids, pair_table, ids, queries, key_side, value_side, attn_out, out_grad, log_norm, bias_all)
    query_grad = lax.psum_scatter(share, "sub", scatter_dimension=3, tiled=True).astype(BF16)
    bias_grad = lax.psum_scatter(running, "row", scatter_dimension=1, tiled=True)
    return (query_grad, key_grad, value_grad, bias_grad)


def solution(mesh):
    return jax.shard_map(
        per_device,
        mesh=mesh,
        in_specs=(
            P("head", ("grp", "row"), None, None),
            P("head", ("grp", "row"), None, "sub"),
            P("head", ("grp", "row"), None, "sub"),
            P("head", ("grp", "row"), None, None),
            P("head", ("grp", "row"), None, None),
            P("head", ("grp", "row"), None),
            P(("grp", "head"), "row", "sub"),
            P("grp"),
            P("grp", None),
        ),
        out_specs=(
            P("head", ("grp", "row"), None, "sub"),
            P("head", ("grp", "row"), None, "sub"),
            P("head", ("grp", "row"), None, "sub"),
            P(("grp", "head"), "row", "sub"),
        ),
        check_vma=False,
    )
```

time: 422 us -> 229 us (0.54); the launches traced: 416 us -> 227 us
  matrix products: 167 us -> 0 us
  Pallas kernels: 0 us -> 73.1 us
  other arithmetic: 69.1 us -> 2.4 us
  local copies, waits for them, and re-layouts: 37.3 us -> 1.58 us
  waiting for transfers between devices: 127 us -> 136 us
    dot_general x61 -> x0, matrix products: 167 us -> none  [the longest x12 68.5 us: score_parts(): jnp.einsum('rdj,rdk->rjk', row_grad, row_value, preferred_element_type=jn...]
    pallas_call x0 -> x1, Pallas kernels: none -> 73.1 us  [per_device(): pl.pallas_call(local_kernel, out_shape=(jax.ShapeDtypeStruct((heads, rows...]
    add x12 -> x0, other arithmetic: 49 us -> none  [step(): updated = carry + bias_part]
    all_gather x1, waiting for transfers between devices: 31.8 us -> 45.5 us  [per_device(): bias_all = lax.all_gather(pair_bias, 'row', axis=1, tiled=True)]
    convert_element_type x14 -> x1, other arithmetic: 13.1 us -> 2.4 us  [per_device(): lax.psum_scatter(share, 'sub', scatter_dimension=3, tiled=True).astype(BF16)]
    sub x12 -> x0, local copies, waits for them, and re-layouts: 8.58 us -> none  [score_parts(): score_grad = attn_prob * (prob_grad - row_delta[:, :, None])]
    broadcast_in_dim x12 -> x0, local copies, waits for them, and re-layouts: 8.2 us -> none  [score_parts(): jnp.where(allowed[:, None, :], jnp.exp(scores - row_norm[:, :, None]), jn...]
    another operation x8 -> x0, local copies, waits for them, and re-layouts: 7.11 us -> none
  transfers between devices with their start and end apart: 5 -> 3, of which waited for: 4 -> 3; matrix products, arithmetic and copies ran while one was open for 33% -> 2% of each run, Pallas kernels for 0% -> 0%
where the time goes in v1:
time: 229 us; the launch traced here: 227 us
  waiting for transfers between devices  136 us (59%)
  Pallas kernels  73.1 us (32%)
  between operations  13.7 us (6%)
  other arithmetic  2.4 us (1%)
    reduce_scatter x1, waiting for transfers between devices, per_device(): lax.psum_scatter(running, 'row', scatter_dimension=1, tiled=True)  78.3 us
    pallas_call x1, Pallas kernels, per_device(): pl.pallas_call(local_kernel, out_shape=(jax.ShapeDtypeStruct((heads, rows...  73.1 us
    all_gather x1, waiting for transfers between devices, per_device(): bias_all = lax.all_gather(pair_bias, 'row', axis=1, tiled=True)  45.5 us
    reduce_scatter x1, waiting for transfers between devices, per_device(): lax.psum_scatter(share, 'sub', scatter_dimension=3, tiled=True).astype(BF16)  10.9 us
  transfers between devices with their start and end apart: 3, of which 3 were waited for; matrix products, arithmetic and copies ran while one was open for 2% of the time, Pallas kernels for 0%

profile of v1, /device:TPU:12, one launch (start us, length us, event | category | flops | bytes accessed | tf_op | source)
XLA Modules:
  0.0 227.0 jit_solution(2729720105091153154)
XLA Ops:
  7.2 0.0 all-gather.2.cloned.1.call-start
  7.2 0.7 all-gather.2.cloned.1.call-update
  7.9 0.0 reduce-scatter.3.cloned.1.call-start
  7.9 1.6 copy.13.n_ref
  9.5 45.5 %all-gather.2.cloned.1.call-done.b_ref = bf16[2,1024,512]{2,1,0:T(8,128)(2,1)} async-done(((bf16[2,256,512]{2,1,0:T(8,128)(2,1)}), bf16[2,1024,512]{2,1,0:T(8,128)(2,1)}) %all-gather.2.cloned.1.call-update) | async-done | bytes 2097168 | tf_op jit(solution)/shard_map/all_gather | solution.py:129
  55.1 73.1 %shard_map.120 = (f32[2,12,32,1024]{3,2,1,0:T(8,128)}, bf16[2,12,32,512]{3,2,1,0:T(8,128)(2,1)}, bf16[2,12,32,512]{3,2,1,0:T(8,128)(2,1)}, f32[2,1024,512]{2,1,0:T(8,128)}) custom-call(s32[1,1024]{1,0:T(1,128)} %bitcast.1, s32[8,8]{1,0:T(8,128)} %table_ref.1, s32[1,1024]{1,0:T(1,128)} %bitcast.2, bf16[2,12,32,1024]{3,2,1,0:T(8,128)(2,1)} %q_ref.1, ...), custom_call_target="tpu_custom_call" | custom-call | tf_op jit(solution)/shard_map/pallas_call | solution.py:133
  128.1 0.0 reduce-scatter.3.cloned.1.call-update
  128.2 0.0 reduce-scatter.5.cloned.1.call-start
  128.2 0.7 reduce-scatter.5.cloned.1.call-update
  128.9 10.9 %reduce-scatter.3.cloned.1.call-done = f32[2,12,32,512]{3,2,1,0:T(8,128)} async-done(((f32[2,12,32,1024]{3,2,1,0:T(8,128)}), f32[2,12,32,512]{3,2,1,0:T(8,128)}) %reduce-scatter.3.cloned.1.call-update) | async-done | bytes 1572880 | tf_op jit(solution)/shard_map/reduce_scatter | solution.py:152
  139.8 2.4 %convert_element_type.3 = bf16[2,12,32,512]{3,2,1,0:T(8,128)(2,1)} convert(f32[2,12,32,512]{3,2,1,0:T(8,128)} %reduce-scatter.3.cloned.1.call-done) | non-fusion elementwise | flops 393216 | bytes 2359296 | tf_op jit(solution)/shard_map/convert_element_type | solution.py:152
  142.2 78.3 %reduce-scatter.5.cloned.1.call-done = f32[2,256,512]{2,1,0:T(8,128)} async-done(((f32[2,1024,512]{2,1,0:T(8,128)}), f32[2,256,512]{2,1,0:T(8,128)}) %reduce-scatter.5.cloned.1.call-update) | async-done | bytes 1048592 | tf_op jit(solution)/shard_map/reduce_scatter | solution.py:153
Async XLA Ops:
  7.2 47.9 %all-gather.2.cloned.1.call-start = ((), (), s32[]{:S(2)}) async-start(), calls=%async_computation.2 | async-start | bytes 2621440 | tf_op jit(solution)/shard_map/all_gather | solution.py:129
  7.9 131.9 %reduce-scatter.3.cloned.1.call-start = ((), (), s32[]{:S(2)}) async-start(), calls=%async_computation.3 | async-start | bytes 4718592 | tf_op jit(solution)/shard_map/reduce_scatter | solution.py:152
  128.2 92.3 %reduce-scatter.5.cloned.1.call-start = ((), (), s32[]{:S(2)}) async-start(), calls=%async_computation.4 | async-start | bytes 5242880 | tf_op jit(solution)/shard_map/reduce_scatter | solution.py:153
Sparse Core Ops, SparseCore 0:
  9.6 45.4 all-gather.1
  128.3 11.4 reduce-scatter.2
  142.7 77.6 reduce-scatter.4

commit v2 on v1

--- a/solution.py
+++ b/solution.py
@@ -12,6 +12,7 @@
 BF16 = jnp.bfloat16
 LOG2E = math.log2(math.e)
 MASKED = -16384.0
+MESH = pl.DeviceIdType.MESH
 
 
 def three_parts(value):
@@ -120,16 +121,246 @@
         dv_ref[h] = dv_acc[...].astype(BF16)
 
 
+def fused_kernel(
+    ids_ref, table_ref, chain_ref, q_ref, k_ref, v_ref, o_ref, do_ref, n_ref, b_ref,
+    dq_ref, dk_ref, dv_ref, db_ref, aug_ref, rhs_ref, bias_ref, dk_acc, dv_acc,
+    shards, totals, leaving, landed, dq_own, dq_peer,
+    shard_send, shard_recv, sum_send, sum_recv, dq_send, dq_recv,
+):
+    heads, rows, head_dim, length = q_ref.shape
+    keys = k_ref.shape[3]
+    blocks, tile = shards.shape[1], shards.shape[2]
+    half_blocks = keys // tile
+    factor = head_dim ** -0.5
+    me, side = lax.axis_index("row"), lax.axis_index("sub")
+    key_first = pl.multiple_of(side * keys, keys)
+    above, below = me < blocks - 1, me > 0
+    prep = (k_ref, v_ref, o_ref, do_ref, n_ref, ids_ref, chain_ref, table_ref, aug_ref, rhs_ref)
+
+    barrier = pltpu.get_barrier_semaphore()
+
+    def greet(device):
+        pl.semaphore_signal(barrier, inc=1, device_id=device, device_id_type=MESH)
+
+    greet({"sub": 1 - side})
+    pl.when(above)(lambda: greet({"row": me + 1}))
+    pl.when(below)(lambda: greet({"row": me - 1}))
+    ends = blocks - 1
+    pl.semaphore_wait(barrier, 1 + (2 * ends - 1 - me) // ends + (me + ends - 1) // ends)
+
+    def shard_copy(h, origin, way, source=None):
+        return pltpu.make_async_remote_copy(
+            src_ref=shards.at[h, origin] if source is None else source,
+            dst_ref=shards.at[h, origin],
+            send_sem=shard_send.at[h, origin, way],
+            recv_sem=shard_recv.at[h, origin],
+            device_id={"row": me + 1 - 2 * way},
+            device_id_type=MESH,
+        )
+
+    def send_own(h):
+        pl.when(above)(lambda: shard_copy(h, me, 0, b_ref.at[h]).start())
+        pl.when(below)(lambda: shard_copy(h, me, 1, b_ref.at[h]).start())
+
+    def arrive(h, distance):
+        @pl.when(me >= distance)
+        def _():
+            shard_copy(h, me - distance, 0).wait_recv()
+            pl.when(above)(lambda: shard_copy(h, me - distance, 0).start())
+
+        @pl.when(me + distance < blocks)
+        def _():
+            shard_copy(h, me + distance, 1).wait_recv()
+            pl.when(below)(lambda: shard_copy(h, me + distance, 1).start())
+
+    def sum_copy(h, block, way):
+        return pltpu.make_async_remote_copy(
+            src_ref=leaving.at[h, block],
+            dst_ref=landed.at[way, h, block],
+            send_sem=sum_send.at[h, block],
+            recv_sem=sum_recv.at[way, h, block],
+            device_id={"row": me + 1 - 2 * way},
+            device_id_type=MESH,
+        )
+
+    def take(h, block, way):
+        sum_copy(h, block, way).wait_recv()
+        totals[h, block] += landed[way, h, block].astype(F32)
+
+    def pass_on(h, distance):
+        @pl.when(me >= distance)
+        def _():
+            block = me - distance
+            pl.when(above)(lambda: take(h, block, 1))
+            leaving[h, block] = totals[h, block].astype(BF16)
+            sum_copy(h, block, 1).start()
+
+        @pl.when(me + distance < blocks)
+        def _():
+            block = me + distance
+            pl.when(below)(lambda: take(h, block, 0))
+            leaving[h, block] = totals[h, block].astype(BF16)
+            sum_copy(h, block, 0).start()
+
+    def finish_sum(h):
+        pl.when(above)(lambda: take(h, me, 1))
+        pl.when(below)(lambda: take(h, me, 0))
+        db_ref[h] = totals[h, me]
+
+    def dq_copy(h, block):
+        return pltpu.make_async_remote_copy(
+            src_ref=dq_own.at[h, block],
+            dst_ref=dq_peer.at[h, block],
+            send_sem=dq_send.at[h, block],
+            recv_sem=dq_recv.at[h, block],
+            device_id={"sub": 1 - side},
+            device_id_type=MESH,
+        )
+
+    def finish_dq(h):
+        for at in range(half_blocks):
+            block = side * half_blocks + at
+            dq_copy(h, block).wait_recv()
+            both = dq_own[h, block] + dq_peer[h, block]
+            dq_ref[h, :, :, at * tile : (at + 1) * tile] = (factor * both).astype(BF16)
+
+    send_own(0)
+    for h in range(heads):
+        shards[h, me] = b_ref[h]
+
+        @pl.loop(0, rows)
+        def _(i):
+            prepare_row(h, i, key_first, me * rows, prep)
+
+    before = [[] for _ in range(heads * blocks + 1)]
+    after = [[] for _ in range(heads * blocks + 1)]
+    last = heads * blocks - 1
+    for h in range(heads):
+        if h:
+            before[h].append(functools.partial(send_own, h))
+        for distance in range(1, blocks):
+            before[h + distance].append(functools.partial(arrive, h, distance))
+            step = last - (heads - 1 - h) - distance
+            after[step].append(functools.partial(pass_on, h, distance))
+        after[last - (heads - 1 - h)].append(functools.partial(finish_sum, h))
+        after[min(last, (h + 1) * blocks)].append(functools.partial(finish_dq, h))
+
+    @pl.loop(0, heads * blocks)
+    def _(step):
+        h = step // blocks
+        turn = (1 - h % 2) * (step % blocks) + (h % 2) * (blocks - 1 - step % blocks)
+        block = 2 * ((me // 2 + turn // 2) % 2) + (me + turn) % 2
+        for at, actions in enumerate(before):
+            if actions:
+                @pl.when(step == at)
+                def _():
+                    for action in actions:
+                        action()
+
+        @pl.when(step % blocks == 0)
+        def _():
+            dk_acc[...] = jnp.zeros_like(dk_acc)
+            dv_acc[...] = jnp.zeros_like(dv_acc)
+
+        columns = pl.ds(pl.multiple_of(block * tile, tile), tile)
+        bias_ref[...] = shards[h, block].astype(F32) * LOG2E
+        acc_ref = totals.at[h, block]
+        acc_ref[...] = jnp.zeros_like(acc_ref)
+        refs = (q_ref, k_ref, do_ref, aug_ref, rhs_ref, bias_ref, acc_ref, None, dk_acc, dv_acc)
+
+        def body(i, carry):
+            dq_own[h, block, i] = row_step(h, i, columns, refs)
+            return carry
+
+        lax.fori_loop(0, rows, body, 0, unroll=2 if rows % 2 == 0 else 1)
+        pl.when(block // half_blocks != side)(lambda: dq_copy(h, block).start())
+
+        @pl.when(step % blocks == blocks - 1)
+        def _():
+            dk_ref[h] = (factor * dk_acc[...]).astype(BF16)
+            dv_ref[h] = dv_acc[...].astype(BF16)
+
+        for at, actions in enumerate(after):
+            if actions:
+                @pl.when(step == at)
+                def _():
+                    for action in actions:
+                        action()
+
+    for h in range(heads):
+        pl.when(above)(lambda: shard_copy(h, me, 0, b_ref.at[h]).wait_send())
+        pl.when(below)(lambda: shard_copy(h, me, 1, b_ref.at[h]).wait_send())
+        for distance in range(1, blocks):
+            @pl.when(me >= distance)
+            def _():
+                pl.when(above)(lambda: shard_copy(h, me - distance, 0).wait_send())
+                sum_copy(h, me - distance, 1).wait_send()
+
+            @pl.when(me + distance < blocks)
+            def _():
+                pl.when(below)(lambda: shard_copy(h, me + distance, 1).wait_send())
+                sum_copy(h, me + distance, 0).wait_send()
+
+        for at in range(half_blocks):
+            dq_copy(h, (1 - side) * half_blocks + at).wait_send()
+
+
+def fused(arrays, ids, pair_table):
+    queries, key_side, pair_bias = arrays[0], arrays[1], arrays[6]
+    heads, rows, head_dim, length = queries.shape
+    keys, tile = key_side.shape[3], pair_bias.shape[1]
+    blocks = length // tile
+    vmem = pl.BlockSpec(memory_space=pltpu.VMEM)
+    smem = pl.BlockSpec(memory_space=pltpu.SMEM)
+    dma = pltpu.SemaphoreType.DMA
+    return pl.pallas_call(
+        fused_kernel,
+        out_shape=(
+            jax.ShapeDtypeStruct((heads, rows, head_dim, keys), BF16),
+            jax.ShapeDtypeStruct((heads, rows, head_dim, keys), BF16),
+            jax.ShapeDtypeStruct((heads, rows, head_dim, keys), BF16),
+            jax.ShapeDtypeStruct((heads, tile, keys), F32),
+        ),
+        in_specs=[smem, smem] + [vmem] * 8,
+        out_specs=(vmem,) * 4,
+        scratch_shapes=[
+            pltpu.VMEM((heads, rows, head_dim, length), BF16),
+            pltpu.VMEM((heads, rows, 4 * head_dim, 2 * keys), BF16),
+            pltpu.VMEM((tile, keys), F32),
+            pltpu.VMEM((rows, head_dim, keys), F32),
+            pltpu.VMEM((rows, head_dim, keys), F32),
+            pltpu.VMEM((heads, blocks, tile, keys), BF16),
+            pltpu.VMEM((heads, blocks, tile, keys), F32),
+            pltpu.VMEM((heads, blocks, tile, keys), BF16),
+            pltpu.VMEM((2, heads, blocks, tile, keys), BF16),
+            pltpu.VMEM((heads, blocks, rows, head_dim, tile), F32),
+            pltpu.VMEM((heads, blocks, rows, head_dim, tile), F32),
+            dma((heads, blocks, 2)),
+            dma((heads, blocks)),
+            dma((heads, blocks)),
+            dma((2, heads, blocks)),
+            dma((heads, blocks)),
+            dma((heads, blocks)),
+        ],
+        compiler_params=pltpu.CompilerParams(
+            vmem_limit_bytes=58 * 1024 * 1024, collective_id=0, has_side_effects=True
+        ),
+    )(ids, pair_table, ids, *arrays)
+
+
 def per_device(
     queries, key_side, value_side, attn_out, out_grad, log_norm, pair_bias, chain_ids, pair_table
 ):
     heads, rows, head_dim, length = queries.shape
     keys = key_side.shape[3]
     tile = min(256, length)
+    ids = chain_ids.reshape(1, length)
+    arrays = (queries, key_side, value_side, attn_out, out_grad, log_norm, pair_bias)
+    if heads == 2 and lax.axis_size("row") == 4 and pair_bias.shape[1] % 128 == 0:
+        return fused(arrays, ids, pair_table)
     bias_all = lax.all_gather(pair_bias, "row", axis=1, tiled=True)
     vmem = pl.BlockSpec(memory_space=pltpu.VMEM)
     smem = pl.BlockSpec(memory_space=pltpu.SMEM)
-    ids = chain_ids.reshape(1, length)
     share, key_grad, value_grad, running = pl.pallas_call(
         local_kernel,
         out_shape=(

time: 229 us -> 101 us (0.44)
  waiting for transfers between devices: 136 us -> 0 us
  Pallas kernels: 73.1 us -> 91.5 us
  between operations: 13.7 us -> 0.66 us
  local copies, waits for them, and re-layouts: 1.58 us -> 6.53 us
  other arithmetic: 2.4 us -> 0 us
    reduce_scatter x2 -> x0, waiting for transfers between devices: 89.2 us -> none  [the longest x1 78.3 us: per_device(): lax.psum_scatter(running, 'row', scatter_dimension=1, tiled=True)]
    all_gather x1 -> x0, waiting for transfers between devices: 45.5 us -> none  [per_device(): bias_all = lax.all_gather(pair_bias, 'row', axis=1, tiled=True)]
    pallas_call x1, Pallas kernels: 73.1 us -> 91.5 us  [fused(): pl.pallas_call(fused_kernel, out_shape=(jax.ShapeDtypeStruct((heads, rows...]
    unnamed x1 -> x11, local copies, waits for them, and re-layouts: 1.58 us -> 6.53 us
    convert_element_type x1 -> x0, other arithmetic: 2.4 us -> none  [per_device(): lax.psum_scatter(share, 'sub', scatter_dimension=3, tiled=True).astype(BF16)]
  transfers between devices with their start and end apart: 3 -> 0, of which waited for: 3 -> 0; matrix products, arithmetic and copies ran while one was open for 2% -> 0% of each run, Pallas kernels for 0% -> 0%
where the time goes in v2:
time: 101 us; the launch traced here: 98.7 us
  Pallas kernels  91.5 us (91%)
  local copies, waits for them, and re-layouts  6.53 us (6%)
    pallas_call x1, Pallas kernels, fused(): pl.pallas_call(fused_kernel, out_shape=(jax.ShapeDtypeStruct((heads, rows...  91.5 us
    unnamed x11, local copies, waits for them, and re-layouts  6.53 us

profile of v2, /device:TPU:12, one launch (start us, length us, event | category | flops | bytes accessed | tf_op | source)
XLA Modules:
  0.0 98.7 jit_solution(1519108142904139131)
XLA Ops:
  0.6 1.6 %copy.13.n_ref = f32[2,12,1024]{2,1,0:T(8,128)} copy(f32[2,12,1024]{2,0,1:T(2,128)} %param.14) | data formatting | bytes 196608 | tf_op args[5]
  2.2 91.5 %shard_map.120 = (bf16[2,12,32,512]{3,2,1,0:T(8,128)(2,1)}, bf16[2,12,32,512]{3,2,1,0:T(8,128)(2,1)}, bf16[2,12,32,512]{3,2,1,0:T(8,128)(2,1)}, f32[2,256,512]{2,1,0:T(8,128)}) custom-call(s32[1,1024]{1,0:T(1,128)} %bitcast.1, s32[8,8]{1,0:T(8,128)} %table_ref.1, s32[1,1024]{1,0:T(1,128)} %bitcast.2, bf16[2,12,32,1024]{3,2,1,0:T(8,128)(2,1)} %q_ref.1, ...), custom_call_target="tpu_custom_call" | custom-call | tf_op jit(solution)/shard_map/pallas_call | solution.py:316
  93.7 0.0 copy-start.2
  93.8 0.0 copy-start.1
  93.8 2.2 %copy.18 = bf16[2,12,32,512]{3,2,1,0:T(8,128)(2,1)} copy(bf16[2,12,32,512]{3,2,1,0:T(8,128)(2,1)} %get-tuple-element.8) | data formatting | bytes 1572864
  96.0 0.0 copy-done.2
  96.0 0.0 copy-start
  96.0 0.9 copy.19
  96.9 0.0 copy-done.1
  96.9 0.9 copy.20
  97.7 0.0 copy-done
  97.7 1.0 copy.21
Async XLA Ops:
  93.7 2.2 %copy-start.2 = (bf16[2,12,32,512]{3,2,1,0:T(8,128)(2,1)S(1)}, bf16[2,12,32,512]{3,2,1,0:T(8,128)(2,1)}, u32[]{:S(2)}) copy-start(bf16[2,12,32,512]{3,2,1,0:T(8,128)(2,1)} %get-tuple-element.9) | copy-start | bytes 2359300
  93.8 3.1 %copy-start.1 = (bf16[2,12,32,512]{3,2,1,0:T(8,128)(2,1)S(1)}, bf16[2,12,32,512]{3,2,1,0:T(8,128)(2,1)}, u32[]{:S(2)}) copy-start(bf16[2,12,32,512]{3,2,1,0:T(8,128)(2,1)} %get-tuple-element.10) | copy-start | bytes 2359300
  96.0 1.8 %copy-start = (f32[2,256,512]{2,1,0:T(8,128)S(1)}, f32[2,256,512]{2,1,0:T(8,128)}, u32[]{:S(2)}) copy-start(f32[2,256,512]{2,1,0:T(8,128)} %get-tuple-element.11) | copy-start | bytes 3145732

commit v3 on v2

--- a/solution.py
+++ b/solution.py
@@ -56,7 +56,7 @@
 def row_step(h, i, columns, refs):
     q_ref, k_ref, do_ref, aug_ref, rhs_ref, bias_ref, acc_ref, dq_ref, dk_ref, dv_ref = refs
     keys = k_ref.shape[3]
-    chunk = min(256, keys)
+    chunk = min(512, keys)
     query = q_ref[h, i, :, columns]
     grad = do_ref[h, i, :, columns]
     left = jnp.concatenate([query, query, grad, aug_ref[h, i, :, columns]], axis=0).T
@@ -232,60 +232,72 @@
         def _(i):
             prepare_row(h, i, key_first, me * rows, prep)
 
-    before = [[] for _ in range(heads * blocks + 1)]
-    after = [[] for _ in range(heads * blocks + 1)]
-    last = heads * blocks - 1
-    for h in range(heads):
-        if h:
-            before[h].append(functools.partial(send_own, h))
-        for distance in range(1, blocks):
-            before[h + distance].append(functools.partial(arrive, h, distance))
-            step = last - (heads - 1 - h) - distance
-            after[step].append(functools.partial(pass_on, h, distance))
-        after[last - (heads - 1 - h)].append(functools.partial(finish_sum, h))
-        after[min(last, (h + 1) * blocks)].append(functools.partial(finish_dq, h))
-
-    @pl.loop(0, heads * blocks)
-    def _(step):
-        h = step // blocks
-        turn = (1 - h % 2) * (step % blocks) + (h % 2) * (blocks - 1 - step % blocks)
+    before = {
+        2: [(arrive, 0, 1)],
+        3: [(send_own, 1)],
+        4: [(arrive, 0, 2)],
+        6: [(arrive, 0, 3), (arrive, 1, 1)],
+        8: [(arrive, 1, 2)],
+        10: [(arrive, 1, 3)],
+    }
+    after = {
+        7: [(pass_on, 0, 3)],
+        9: [(pass_on, 0, 2)],
+        11: [(pass_on, 1, 3), (pass_on, 0, 1)],
+        13: [(pass_on, 1, 2)],
+        14: [(finish_dq, 0)],
+        15: [(pass_on, 1, 1), (finish_sum, 0), (finish_dq, 1), (finish_sum, 1)],
+    }
+
+    def run(plan, half_step):
+        for at, actions in plan.items():
+            @pl.when(half_step == at)
+            def _():
+                for action, *what in actions:
+                    action(*what)
+
+    half_rows = rows // 2
+
+    @pl.loop(0, 2 * heads * blocks)
+    def _(half_step):
+        step = half_step // 2
+        h, turn = step // blocks, step % blocks
+        turn = (1 - h) * turn + h * (2 * (1 - turn // 2) + (turn + turn // 2) % 2)
         block = 2 * ((me // 2 + turn // 2) % 2) + (me + turn) % 2
-        for at, actions in enumerate(before):
-            if actions:
-                @pl.when(step == at)
-                def _():
-                    for action in actions:
-                        action()
-
-        @pl.when(step % blocks == 0)
+        run(before, half_step)
+
+        @pl.when(half_step % (2 * blocks) == 0)
         def _():
             dk_acc[...] = jnp.zeros_like(dk_acc)
             dv_acc[...] = jnp.zeros_like(dv_acc)
 
         columns = pl.ds(pl.multiple_of(block * tile, tile), tile)
-        bias_ref[...] = shards[h, block].astype(F32) * LOG2E
         acc_ref = totals.at[h, block]
-        acc_ref[...] = jnp.zeros_like(acc_ref)
+
+        @pl.when(half_step % 2 == 0)
+        def _():
+            bias_ref[...] = shards[h, block].astype(F32) * LOG2E
+            acc_ref[...] = jnp.zeros_like(acc_ref)
+
         refs = (q_ref, k_ref, do_ref, aug_ref, rhs_ref, bias_ref, acc_ref, None, dk_acc, dv_acc)
+        first = half_step % 2 * half_rows
 
         def body(i, carry):
-            dq_own[h, block, i] = row_step(h, i, columns, refs)
+            dq_own[h, block, first + i] = row_step(h, first + i, columns, refs)
             return carry
 
-        lax.fori_loop(0, rows, body, 0, unroll=2 if rows % 2 == 0 else 1)
-        pl.when(block // half_blocks != side)(lambda: dq_copy(h, block).start())
-
-        @pl.when(step % blocks == blocks - 1)
+        lax.fori_loop(0, half_rows, body, 0, unroll=6 if half_rows % 6 == 0 else 1)
+
+        @pl.when((half_step % 2 == 1) & (block // half_blocks != side))
+        def _():
+            dq_copy(h, block).start()
+
+        @pl.when(half_step % (2 * blocks) == 2 * blocks - 1)
         def _():
             dk_ref[h] = (factor * dk_acc[...]).astype(BF16)
             dv_ref[h] = dv_acc[...].astype(BF16)
 
-        for at, actions in enumerate(after):
-            if actions:
-                @pl.when(step == at)
-                def _():
-                    for action in actions:
-                        action()
+        run(after, half_step)
 
     for h in range(heads):
         pl.when(above)(lambda: shard_copy(h, me, 0, b_ref.at[h]).wait_send())
@@ -356,7 +368,7 @@
     tile = min(256, length)
     ids = chain_ids.reshape(1, length)
     arrays = (queries, key_side, value_side, attn_out, out_grad, log_norm, pair_bias)
-    if heads == 2 and lax.axis_size("row") == 4 and pair_bias.shape[1] % 128 == 0:
+    if heads == 2 and rows % 2 == 0 and lax.axis_size("row") == 4 and pair_bias.shape[1] % 128 == 0:
         return fused(arrays, ids, pair_table)
     bias_all = lax.all_gather(pair_bias, "row", axis=1, tiled=True)
     vmem = pl.BlockSpec(memory_space=pltpu.VMEM)

time: 101 us -> 83.2 us (0.82); the launches traced: 98.7 us -> 83 us
  Pallas kernels: 91.5 us -> 75.9 us
    pallas_call x1, Pallas kernels: 91.5 us -> 75.9 us  [fused(): pl.pallas_call(fused_kernel, out_shape=(jax.ShapeDtypeStruct((heads, rows...]
where the time goes in v3:
time: 83.2 us; the launch traced here: 83 us
  Pallas kernels  75.9 us (91%)
  local copies, waits for them, and re-layouts  6.53 us (8%)
    pallas_call x1, Pallas kernels, fused(): pl.pallas_call(fused_kernel, out_shape=(jax.ShapeDtypeStruct((heads, rows...  75.9 us
    unnamed x11, local copies, waits for them, and re-layouts  6.53 us

profile of v3, /device:TPU:12, one launch (start us, length us, event | category | flops | bytes accessed | tf_op | source)
XLA Modules:
  0.0 83.0 jit_solution(12324519050115473676)
XLA Ops:
  0.6 1.6 %copy.13.n_ref = f32[2,12,1024]{2,1,0:T(8,128)} copy(f32[2,12,1024]{2,0,1:T(2,128)} %param.14) | data formatting | bytes 196608 | tf_op args[5]
  2.2 75.9 %shard_map.120 = (bf16[2,12,32,512]{3,2,1,0:T(8,128)(2,1)}, bf16[2,12,32,512]{3,2,1,0:T(8,128)(2,1)}, bf16[2,12,32,512]{3,2,1,0:T(8,128)(2,1)}, f32[2,256,512]{2,1,0:T(8,128)}) custom-call(s32[1,1024]{1,0:T(1,128)} %bitcast.1, s32[8,8]{1,0:T(8,128)} %table_ref.1, s32[1,1024]{1,0:T(1,128)} %bitcast.2, bf16[2,12,32,1024]{3,2,1,0:T(8,128)(2,1)} %q_ref.1, ...), custom_call_target="tpu_custom_call" | custom-call | tf_op jit(solution)/shard_map/pallas_call | solution.py:328
  78.1 0.0 copy-start.2
  78.1 0.0 copy-start.1
  78.1 2.2 %copy.18 = bf16[2,12,32,512]{3,2,1,0:T(8,128)(2,1)} copy(bf16[2,12,32,512]{3,2,1,0:T(8,128)(2,1)} %get-tuple-element.8) | data formatting | bytes 1572864
  80.3 0.0 copy-done.2
  80.3 0.0 copy-start
  80.3 0.9 %copy.19 = bf16[2,12,32,512]{3,2,1,0:T(8,128)(2,1)} copy(bf16[2,12,32,512]{3,2,1,0:T(8,128)(2,1)S(1)} %copy-done.2) | data formatting | bytes 1572864
  81.2 0.0 copy-done.1
  81.2 0.9 %copy.20 = bf16[2,12,32,512]{3,2,1,0:T(8,128)(2,1)} copy(bf16[2,12,32,512]{3,2,1,0:T(8,128)(2,1)S(1)} %copy-done.1) | data formatting | bytes 1572864
  82.1 0.0 copy-done
  82.1 1.0 %copy.21 = f32[2,256,512]{2,1,0:T(8,128)} copy(f32[2,256,512]{2,1,0:T(8,128)S(1)} %copy-done) | data formatting | bytes 2097152
Async XLA Ops:
  78.1 2.2 %copy-start.2 = (bf16[2,12,32,512]{3,2,1,0:T(8,128)(2,1)S(1)}, bf16[2,12,32,512]{3,2,1,0:T(8,128)(2,1)}, u32[]{:S(2)}) copy-start(bf16[2,12,32,512]{3,2,1,0:T(8,128)(2,1)} %get-tuple-element.9) | copy-start | bytes 2359300
  78.1 3.1 %copy-start.1 = (bf16[2,12,32,512]{3,2,1,0:T(8,128)(2,1)S(1)}, bf16[2,12,32,512]{3,2,1,0:T(8,128)(2,1)}, u32[]{:S(2)}) copy-start(bf16[2,12,32,512]{3,2,1,0:T(8,128)(2,1)} %get-tuple-element.10) | copy-start | bytes 2359300
  80.3 1.8 %copy-start = (f32[2,256,512]{2,1,0:T(8,128)S(1)}, f32[2,256,512]{2,1,0:T(8,128)}, u32[]{:S(2)}) copy-start(f32[2,256,512]{2,1,0:T(8,128)} %get-tuple-element.11) | copy-start | bytes 3145732

commit v4 on v3

--- a/solution.py
+++ b/solution.py
@@ -233,10 +233,11 @@
             prepare_row(h, i, key_first, me * rows, prep)
 
     before = {
-        2: [(arrive, 0, 1)],
-        3: [(send_own, 1)],
+        1: [(arrive, 0, 1)],
+        2: [(send_own, 1)],
         4: [(arrive, 0, 2)],
-        6: [(arrive, 0, 3), (arrive, 1, 1)],
+        5: [(arrive, 1, 1)],
+        6: [(arrive, 0, 3)],
         8: [(arrive, 1, 2)],
         10: [(arrive, 1, 3)],
     }

time: 83.2 us -> 82.5 us (level)
  no operation moved by 1% of the time
where the time goes in v4:
time: 82.5 us; the launch traced here: 82.4 us
  Pallas kernels  75.2 us (91%)
  local copies, waits for them, and re-layouts  6.53 us (8%)
    pallas_call x1, Pallas kernels, fused(): pl.pallas_call(fused_kernel, out_shape=(jax.ShapeDtypeStruct((heads, rows...  75.2 us
    unnamed x11, local copies, waits for them, and re-layouts  6.53 us

profile of v4, /device:TPU:12, one launch (start us, length us, event | category | flops | bytes accessed | tf_op | source)
XLA Modules:
  0.0 82.4 jit_solution(1898216464699821251)
XLA Ops:
  0.6 1.6 %copy.13.n_ref = f32[2,12,1024]{2,1,0:T(8,128)} copy(f32[2,12,1024]{2,0,1:T(2,128)} %param.14) | data formatting | bytes 196608 | tf_op args[5]
  2.2 75.2 %shard_map.120 = (bf16[2,12,32,512]{3,2,1,0:T(8,128)(2,1)}, bf16[2,12,32,512]{3,2,1,0:T(8,128)(2,1)}, bf16[2,12,32,512]{3,2,1,0:T(8,128)(2,1)}, f32[2,256,512]{2,1,0:T(8,128)}) custom-call(s32[1,1024]{1,0:T(1,128)} %bitcast.1, s32[8,8]{1,0:T(8,128)} %table_ref.1, s32[1,1024]{1,0:T(1,128)} %bitcast.2, bf16[2,12,32,1024]{3,2,1,0:T(8,128)(2,1)} %q_ref.1, ...), custom_call_target="tpu_custom_call" | custom-call | tf_op jit(solution)/shard_map/pallas_call | solution.py:329
  77.4 0.0 copy-start.2
  77.4 0.0 copy-start.1
  77.4 2.2 %copy.18 = bf16[2,12,32,512]{3,2,1,0:T(8,128)(2,1)} copy(bf16[2,12,32,512]{3,2,1,0:T(8,128)(2,1)} %get-tuple-element.8) | data formatting | bytes 1572864
  79.6 0.0 copy-done.2
  79.6 0.0 copy-start
  79.6 0.9 %copy.19 = bf16[2,12,32,512]{3,2,1,0:T(8,128)(2,1)} copy(bf16[2,12,32,512]{3,2,1,0:T(8,128)(2,1)S(1)} %copy-done.2) | data formatting | bytes 1572864
  80.5 0.0 copy-done.1
  80.5 0.9 %copy.20 = bf16[2,12,32,512]{3,2,1,0:T(8,128)(2,1)} copy(bf16[2,12,32,512]{3,2,1,0:T(8,128)(2,1)S(1)} %copy-done.1) | data formatting | bytes 1572864
  81.4 0.0 copy-done
  81.4 1.0 %copy.21 = f32[2,256,512]{2,1,0:T(8,128)} copy(f32[2,256,512]{2,1,0:T(8,128)S(1)} %copy-done) | data formatting | bytes 2097152
Async XLA Ops:
  77.4 2.2 %copy-start.2 = (bf16[2,12,32,512]{3,2,1,0:T(8,128)(2,1)S(1)}, bf16[2,12,32,512]{3,2,1,0:T(8,128)(2,1)}, u32[]{:S(2)}) copy-start(bf16[2,12,32,512]{3,2,1,0:T(8,128)(2,1)} %get-tuple-element.9) | copy-start | bytes 2359300
  77.4 3.1 %copy-start.1 = (bf16[2,12,32,512]{3,2,1,0:T(8,128)(2,1)S(1)}, bf16[2,12,32,512]{3,2,1,0:T(8,128)(2,1)}, u32[]{:S(2)}) copy-start(bf16[2,12,32,512]{3,2,1,0:T(8,128)(2,1)} %get-tuple-element.10) | copy-start | bytes 2359300
  79.6 1.8 %copy-start = (f32[2,256,512]{2,1,0:T(8,128)S(1)}, f32[2,256,512]{2,1,0:T(8,128)}, u32[]{:S(2)}) copy-start(f32[2,256,512]{2,1,0:T(8,128)} %get-tuple-element.11) | copy-start | bytes 3145732
